TPU v7x, 512 devices: a whole 4x4x16 slice. The times are simulated.
512 devices in a mesh: ep: 128 (over x, z, core), tp: 4 (over y).
Axes of the slice: x: 4, y: 4, z: 16, core: 2. Of those that a mesh axis runs over, the one named last changes fastest.
Arguments:
- grad_out: bfloat16 [16384, 2048], P('ep'), may hold values from -6 to 6
- expert_ids: int32 [16384, 10], P('ep'), may hold values from 0 to 255, all different within a row; in each aligned block of 128 rows (0 to 127, 128 to 255, ...) at most 6 rows name the same one
- gate_values: float32 [16384, 10], P('ep'), may hold values from 0.04 to 0.24
- saved_gate_up: bfloat16 [256, 2, 768, 512], P('ep', None, None, 'tp'), may hold values from -6 to 6
- expert_gate_up: bfloat16 [256, 2, 2048, 512], P('ep', None, None, 'tp'), may hold values from -0.25 to 0.25
- expert_down: bfloat16 [256, 512, 2048], P('ep', 'tp'), may hold values from -0.125 to 0.125
- shared_saved: bfloat16 [2, 16384, 512], P(None, 'ep', 'tp'), may hold values from -6 to 6
- shared_gate_up: bfloat16 [2, 2048, 512], P(None, 'ep', 'tp'), may hold values from -0.25 to 0.25
- shared_down: bfloat16 [512, 2048], P('tp', 'ep'), may hold values from -0.125 to 0.125
Outputs:
- grad_in: bfloat16 [16384, 2048], P('ep', 'tp')
Inputs may be any that keep to these rules, and one draw needn't show every extreme that they name: `expert_ids`: each token names 10 different experts; among the 128 tokens of one index of ep no expert is named more than 6 times, a bound that some block reaches.
All inputs are finite; a program needn't handle non-finite values.
Results may differ from a plain program's by a relative error of at most 0.0051.
Values may be sent and summed in bfloat16 or wider, within the bound.
A program may use at most 128 MiB of HBM per device.

v0:
```python
import jax
import jax.numpy as jnp
from jax import lax
from jax.sharding import PartitionSpec as P


def activation_grad(hidden_grad, saved_pair):
    gate_pre = saved_pair[0].astype(jnp.float32)
    up_pre = saved_pair[1].astype(jnp.float32)
    squash = jax.nn.sigmoid(gate_pre)
    gate_grad = (hidden_grad * up_pre * squash * (1.0 + gate_pre * (1.0 - squash))).astype(
        jnp.bfloat16
    )
    up_grad = (hidden_grad * gate_pre * squash).astype(jnp.bfloat16)
    return (gate_grad, up_grad)


def contract_last(left_mat, right_mat):
    return lax.dot_general(
        left_mat, right_mat, (((1,), (1,)), ((), ())), preferred_element_type=jnp.float32
    )


def combine_rows(back_rows, slot_grid, gate_values):
    picked = back_rows[slot_grid]
    return jnp.sum(gate_values[:, :, None] * picked.astype(jnp.float32), axis=1)


def shards(
    grad_out,
    expert_ids,
    gate_values,
    saved_gate_up,
    expert_gate_up,
    expert_down,
    shared_saved,
    shared_gate_up,
    shared_down,
):
    ep_count = lax.axis_size("ep")
    local_experts = expert_down.shape[0]
    all_experts = local_experts * ep_count
    capacity = saved_gate_up.shape[2] // ep_count
    hidden_local = saved_gate_up.shape[3]
    tokens_here, top_count = expert_ids.shape
    feature_width = grad_out.shape[1]
    flat_ids = expert_ids.reshape(-1)
    one_hot = (flat_ids[:, None] == jnp.arange(all_experts, dtype=jnp.int32)[None, :]).astype(
        jnp.int32
    )
    slot_rank = jnp.sum((jnp.cumsum(one_hot, axis=0) - one_hot) * one_hot, axis=1)
    slot_index = flat_ids * capacity + slot_rank
    owner_token = (
        jnp.zeros((all_experts * capacity,), jnp.int32)
        .at[slot_index]
        .set(jnp.arange(tokens_here * top_count, dtype=jnp.int32) // top_count)
    )
    filled = jnp.zeros((all_experts * capacity,), jnp.bool_).at[slot_index].set(True)
    outgoing = jnp.where(filled[:, None], grad_out[owner_token], jnp.zeros((), jnp.bfloat16))
    outgoing = outgoing.reshape(ep_count, local_experts, capacity, feature_width)
    arrived = lax.all_to_all(outgoing, "ep", split_axis=0, concat_axis=0, tiled=True)
    hidden_grad = jnp.einsum(
        "pecd,efd->epcf", arrived, expert_down, preferred_element_type=jnp.float32
    )
    saved_gate = saved_gate_up[:, 0].reshape(local_experts, ep_count, capacity, hidden_local)
    saved_up = saved_gate_up[:, 1].reshape(local_experts, ep_count, capacity, hidden_local)
    gate_grad, up_grad = activation_grad(hidden_grad, (saved_gate, saved_up))
    partial_value = jnp.einsum(
        "epcf,edf->pecd", gate_grad, expert_gate_up[:, 0], preferred_element_type=jnp.float32
    ) + jnp.einsum(
        "epcf,edf->pecd", up_grad, expert_gate_up[:, 1], preferred_element_type=jnp.float32
    )
    going_back = partial_value.astype(jnp.bfloat16)
    slot_grid = slot_index.reshape(tokens_here, top_count)
    shared_hidden = contract_last(grad_out, lax.all_gather(shared_down, "ep", axis=1, tiled=True))
    shared_gate_grad, shared_up_grad = activation_grad(shared_hidden, shared_saved)
    shard_piece = lax.all_gather(shared_gate_up, "ep", axis=1, tiled=True)
    shared_part = contract_last(shared_gate_grad, shard_piece[0]) + contract_last(
        shared_up_grad, shard_piece[1]
    )
    returned = lax.all_to_all(going_back, "ep", split_axis=0, concat_axis=0, tiled=True)
    back_rows = returned.reshape(all_experts * capacity, feature_width)
    routed = combine_rows(back_rows, slot_grid, gate_values)
    summed = lax.psum_scatter(routed + shared_part, "tp", scatter_dimension=1, tiled=True)
    return summed.astype(jnp.bfloat16)


def solution(mesh):
    in_specs = (
        P("ep", None),
        P("ep", None),
        P("ep", None),
        P("ep", None, None, "tp"),
        P("ep", None, None, "tp"),
        P("ep", "tp", None),
        P(None, "ep", "tp"),
        P(None, "ep", "tp"),
        P("tp", "ep"),
    )
    out_specs = P("ep", "tp")
    return jax.shard_map(shards, mesh=mesh, in_specs=in_specs, out_specs=out_specs, check_vma=False)
```

profile of v0, /device:TPU:1, one launch (start us, length us, event | category | flops | bytes accessed | tf_op | source)
XLA Modules:
  0.0 860.1 jit_solution(14724220900248237846)
XLA Ops:
  6.5 0.0 copy-start
  6.5 0.0 copy-start.2
  6.5 0.9 copy.47
  7.5 0.1 eq.29
  7.6 0.1 eq.25
  7.7 0.1 copy.50
  7.9 0.3 fusion.4
  8.2 0.0 copy-start.3
  8.2 1.3 copy-done.3
  9.6 1.8 broadcast_add_fusion
  11.4 0.8 copy.51
  12.2 0.5 fusion.7
  12.7 0.1 reduce_sum.24
  12.8 0.1 mul.67
  13.0 5.2 scatter_custom_fusion.1
  18.3 0.0 copy-done.2
  18.3 7.1 gather_fusion
  25.4 10.9 %gather.9 = bf16[128,2,6,2048]{3,2,1,0:T(8,128)(2,1)} reshape(bf16[1536,2048]{1,0:T(8,128)(2,1)} %gather_fusion) | data formatting | bytes 12582912 | tf_op jit(solution)/shard_map/gather | solution.py:59
  36.3 22.2 %scatter_custom_fusion = pred[1536]{0:T(1024)(128)(4,1)S(1)} fusion(s32[1280]{0:T(1024)S(1)} %fusion.44, pred[1280]{0:T(1024)(128)(4,1)S(1)} %broadcast.68, pred[]{:T(512)} %constant.12.clone.1), kind=kCustom, calls=%fused_computation.78 | custom fusion | bytes 1537 | tf_op jit(solution)/shard_map/scatter | solution.py:58
  58.6 0.2 broadcast_in_dim.33
  58.8 7.5 broadcast_select_fusion
  66.2 10.4 %copy.52 = bf16[128,2,6,2048]{3,1,2,0:T(2,128)(2,1)} copy(bf16[128,2,6,2048]{3,2,1,0:T(8,128)(2,1)} %broadcast_select_fusion) | data formatting | bytes 12582912 | tf_op jit(solution)/shard_map/jit(_where)/select_n | solution.py:59
  76.7 0.0 copy-start.5
  76.7 20.9 %all-to-all-start = ((bf16[128,2,6,2048]{3,1,2,0:T(2,128)(2,1)}), bf16[128,2,6,2048]{3,1,2,0:T(2,128)(2,1)}, u32[]{:S(2)}, u32[]{:S(2)}) async-start(bf16[128,2,6,2048]{3,1,2,0:T(2,128)(2,1)} %copy.52), calls=%async_computation | async-start | bytes 12582912 | tf_op jit(solution)/shard_map/all_to_all | solution.py:61
  97.6 0.0 copy-done.5
  97.6 0.1 slice_convert_fusion
  97.7 0.6 copy.56
  98.4 0.6 copy.54
  99.0 273.1 %all-to-all-done = bf16[128,2,6,2048]{3,1,2,0:T(2,128)(2,1)} async-done(((bf16[128,2,6,2048]{3,1,2,0:T(2,128)(2,1)}), bf16[128,2,6,2048]{3,1,2,0:T(2,128)(2,1)}, u32[]{:S(2)}, u32[]{:S(2)}) %all-to-all-start) | async-done | bytes 6291488 | tf_op jit(solution)/shard_map/all_to_all | solution.py:61
  372.1 0.0 copy-done
  372.1 0.0 copy-start.4
  372.1 6.5 fusion.1
  378.5 0.0 copy-done.4
  378.5 1.8 fusion.9
  380.4 5.7 fusion
  386.1 12.7 %copy.62 = bf16[128,2,6,2048]{3,1,2,0:T(2,128)(2,1)} copy(bf16[128,2,6,2048]{3,0,2,1:T(8,128)(2,1)} %fusion) | data formatting | bytes 12582912 | tf_op jit(solution)/shard_map/convert_element_type | solution.py:73
  398.8 0.0 copy-start.7
  398.8 0.0 copy-start.8
  398.8 0.0 copy-start.6
  398.8 13.4 %all-to-all-start.1 = ((bf16[128,2,6,2048]{3,1,2,0:T(2,128)(2,1)}), bf16[128,2,6,2048]{3,1,2,0:T(2,128)(2,1)}, u32[]{:S(2)}, u32[]{:S(2)}) async-start(bf16[128,2,6,2048]{3,1,2,0:T(2,128)(2,1)} %copy.62), calls=%async_computation.1 | async-start | bytes 12582912 | tf_op jit(solution)/shard_map/all_to_all | solution.py:81
  412.3 0.0 all-gather.2.cloned.1.call-start
  412.3 0.7 all-gather.2.cloned.1.call-update
  413.0 0.0 reduce-scatter.2.cloned.1.call-start
  413.0 0.1 reshape.84
  413.2 0.0 copy-done.7
  413.2 0.1 copy.46
  413.3 0.0 copy-done.8
  413.3 349.9 %all_gather.6 = bf16[128,2048]{0,1:T(8,128)(2,1)S(1)} all-gather(bf16[128,16]{0,1:T(8,128)(2,1)S(1)} %copy-done.8), channel_id=1, replica_groups=mesh['ep'=128,'tp'=4] {'ep'}, dimensions={1}, use_global_device_ids=true | all-gather | bytes 528384 | tf_op jit(solution)/shard_map/all_gather | solution.py:75
  763.3 0.3 fusion.53
  763.6 0.0 all-gather.2.cloned.1.call-done
  763.6 0.0 copy-done.6
  763.6 1.3 fusion.18
  764.9 0.0 all-to-all-done.1
  765.0 10.4 %copy.63 = bf16[128,2,6,2048]{3,2,1,0:T(8,128)(2,1)} copy(bf16[128,2,6,2048]{3,1,2,0:T(2,128)(2,1)} %all-to-all-done.1) | data formatting | bytes 12582912 | tf_op jit(solution)/shard_map/all_to_all | solution.py:81
  775.4 11.3 %reshape.69 = bf16[1536,2048]{1,0:T(8,128)(2,1)} reshape(bf16[128,2,6,2048]{3,2,1,0:T(8,128)(2,1)} %copy.63) | data formatting | bytes 12582912 | tf_op jit(solution)/shard_map/reshape | solution.py:82
  786.6 14.4 %gather_fusion.1 = bf16[1280,2048]{1,0:T(8,128)(2,1)} fusion(bf16[1536,2048]{1,0:T(8,128)(2,1)} %reshape.69, s32[2048]{0:T(1024)S(1)} %pad_clamp_fusion), kind=kCustom, calls=%fused_computation.1 | custom fusion | bytes 10490880 | tf_op jit(solution)/shard_map/gather | solution.py:25
  801.1 10.4 %reshape.109 = f32[128,10,2048]{2,1,0:T(8,128)} reshape(bf16[1280,2048]{1,0:T(8,128)(2,1)} %gather_fusion.1) | data formatting | bytes 15728640 | tf_op jit(solution)/shard_map/convert_element_type | solution.py:26
  811.5 0.0 copy-start.1
  811.5 9.6 %multiply_reduce_fusion = f32[128,2048]{1,0:T(8,128)S(1)} fusion(f32[128,10,2048]{2,1,0:T(8,128)} %reshape.109, f32[128,10]{1,0:T(8,128)S(1)} %copy.46), kind=kLoop, calls=%fused_computation.4 | loop fusion | flops 4980736 | bytes 11539456 | tf_op jit(solution)/shard_map/reduce_sum | solution.py:26
  821.1 2.3 fusion.3
  823.4 0.0 reduce-scatter.2.cloned.1.call-update
  823.4 27.8 %reduce-scatter.2.cloned.1.call-done = f32[128,512]{1,0:T(8,128)} async-done(((f32[128,2048]{1,0:T(8,128)}), f32[128,512]{1,0:T(8,128)}) %reduce-scatter.2.cloned.1.call-update) | async-done | bytes 262160 | tf_op jit(solution)/shard_map/reduce_scatter | solution.py:84
  851.2 1.6 convert_element_type.72
  852.8 0.0 copy-done.1
  (9 shorter events, 0.1 us)
Async XLA Ops:
  6.5 365.5 %copy-start = (bf16[2,128,2048]{2,1,0:T(8,128)(2,1)S(1)}, bf16[2,128,2048]{2,1,0:T(8,128)(2,1)}, u32[]{:S(2)}) copy-start(bf16[2,128,2048]{2,1,0:T(8,128)(2,1)} %param.14) | copy-start | bytes 3145732
  6.5 11.7 %copy-start.2 = (bf16[128,2048]{1,0:T(8,128)(2,1)S(1)}, bf16[128,2048]{1,0:T(8,128)(2,1)}, u32[]{:S(2)}) copy-start(bf16[128,2048]{1,0:T(8,128)(2,1)} %param.9) | copy-start | bytes 1572868
  8.2 1.4 copy-start.3
  76.7 20.9 %copy-start.5 = (bf16[2,2,768,128]{3,2,1,0:T(8,128)(2,1)S(1)}, bf16[2,2,768,128]{3,2,1,0:T(8,128)(2,1)}, u32[]{:S(2)}) copy-start(bf16[2,2,768,128]{3,2,1,0:T(8,128)(2,1)} %param.12) | copy-start | bytes 2359300
  76.7 295.4 %all-to-all-start = ((bf16[128,2,6,2048]{3,1,2,0:T(2,128)(2,1)}), bf16[128,2,6,2048]{3,1,2,0:T(2,128)(2,1)}, u32[]{:S(2)}, u32[]{:S(2)}) async-start(bf16[128,2,6,2048]{3,1,2,0:T(2,128)(2,1)} %copy.52), calls=%async_computation | async-start | bytes 12582912 | tf_op jit(solution)/shard_map/all_to_all | solution.py:61
  372.1 6.5 copy-start.4
  398.8 14.4 %copy-start.7 = (f32[128,10]{0,1:T(8,128)S(1)}, f32[128,10]{0,1:T(8,128)}, u32[]{:S(2)}) copy-start(f32[128,10]{0,1:T(8,128)} %param.11) | copy-start | bytes 15364
  398.8 14.5 %copy-start.8 = (bf16[128,16]{0,1:T(8,128)(2,1)S(1)}, bf16[128,16]{0,1:T(8,128)(2,1)}, u32[]{:S(2)}) copy-start(bf16[128,16]{0,1:T(8,128)(2,1)} %param.17) | copy-start | bytes 12292
  398.8 364.8 %copy-start.6 = (bf16[2,128,128]{2,1,0:T(8,128)(2,1)S(1)}, bf16[2,128,128]{2,1,0:T(8,128)(2,1)}, u32[]{:S(2)}) copy-start(bf16[2,128,128]{2,1,0:T(8,128)(2,1)} %param.15) | copy-start | bytes 196612
  398.8 366.1 %all-to-all-start.1 = ((bf16[128,2,6,2048]{3,1,2,0:T(2,128)(2,1)}), bf16[128,2,6,2048]{3,1,2,0:T(2,128)(2,1)}, u32[]{:S(2)}, u32[]{:S(2)}) async-start(bf16[128,2,6,2048]{3,1,2,0:T(2,128)(2,1)} %copy.62), calls=%async_computation.1 | async-start | bytes 12582912 | tf_op jit(solution)/shard_map/all_to_all | solution.py:81
  412.3 351.3 %all-gather.2.cloned.1.call-start = ((), (), s32[]{:S(2)}) async-start(), calls=%async_computation.3 | async-start | bytes 1056768 | tf_op jit(solution)/shard_map/all_gather | solution.py:77
  413.0 438.2 %reduce-scatter.2.cloned.1.call-start = ((), (), s32[]{:S(2)}) async-start(), calls=%async_computation.4 | async-start | bytes 1310720 | tf_op jit(solution)/shard_map/reduce_scatter | solution.py:84
  811.5 41.4 %copy-start.1 = (bf16[2,128,2048]{2,1,0:T(8,128)(2,1)S(1)}, bf16[2,128,2048]{2,1,0:T(8,128)(2,1)}, u32[]{:S(2)}) copy-start(bf16[2,128,2048]{2,1,0:T(8,128)(2,1)} %param.14) | copy-start | bytes 3145732
Sparse Core Ops, SparseCore 0:
  416.1 182.9 all-gather.1
  823.6 27.6 reduce-scatter.1
where the time goes:
time: 864 us; the launch traced here: 860 us
  blocking collectives  350 us (41%)
  waiting for transfers between devices  302 us (35%)
  local copies, waits for them, and re-layouts  121 us (14%)
  starting transfers between devices  34.4 us (4%)
  other arithmetic  21.5 us (2%)
  matrix products  18 us (2%)
  between operations  14.1 us (2%)
    all_gather x1, blocking collectives, shards(): lax.all_gather(shared_down, 'ep', axis=1, tiled=True)  350 us
    all_to_all x1, waiting for transfers between devices, shards(): lax.all_to_all(outgoing, 'ep', split_axis=0, concat_axis=0, tiled=True)  273 us
    reduce_scatter x1, waiting for transfers between devices, shards(): lax.psum_scatter(routed + shared_part, 'tp', scatter_dimension=1, tiled=T...  27.8 us
    scatter x1, local copies, waits for them, and re-layouts, shards(): jnp.zeros((all_experts * capacity,), jnp.bool_).at[slot_index].set(True)  22.2 us
    all_to_all x1, starting transfers between devices, shards(): lax.all_to_all(outgoing, 'ep', split_axis=0, concat_axis=0, tiled=True)  20.9 us
    gather x2, local copies, waits for them, and re-layouts, shards(): grad_out[owner_token]  18 us
  transfers between devices with their start and end apart: 4, of which 2 were waited for; matrix products, arithmetic and copies ran while one was open for 0% of the time, Pallas kernels for 0%

commit v1 on v0

v1 whole, which is shorter than its diff:
```python
import functools

import jax
import jax.numpy as jnp
from jax import lax
from jax.experimental import pallas as pl
from jax.experimental.pallas import tpu as pltpu
from jax.sharding import PartitionSpec as P

BF = jnp.bfloat16
F32 = jnp.float32
NX, NZ, NC, NY = 4, 16, 2, 4
PEERS = NX * NC
TOK = 128
CAP = 6
TOP = 10
DQ = 512
HQ = 128
NE = 2
GROUPS = 2
SPAN = NZ // GROUPS
SROWS = SPAN * CAP
QN = PEERS * NE
ROWS = PEERS * SROWS
HOME = 3


def dot_nt(a, b):
    return lax.dot_general(a, b, (((1,), (1,)), ((), ())), preferred_element_type=F32)


def dot_nn(a, b):
    return lax.dot_general(a, b, (((1,), (0,)), ((), ())), preferred_element_type=F32)


def dot_tn(a, b):
    return lax.dot_general(a, b, (((0,), (0,)), ((), ())), preferred_element_type=F32)


def act_grad(h, g, u):
    g = g.astype(F32)
    u = u.astype(F32)
    s = jax.nn.sigmoid(g)
    return (h * u * s * (1.0 + g * (1.0 - s))).astype(BF), (h * g * s).astype(BF)


def kernel(
    x_in, meta_in, sw_in, saved, gu, down, ssaved, out,
    XG, MG, SW, SEL, WTH, WTL, SB, R1, W1, W2, SVI, SVP, HO, HS, HR, G, OB, BK, PT, ZS, ZR, XF, SHO, SP, SR,
    ssem, rsem, lsem,
):
    ep = lax.axis_index("ep")
    y = lax.axis_index("tp")
    c = lax.rem(ep, NC)
    z = lax.rem(lax.div(ep, NC), NZ)
    x = lax.div(ep, NC * NZ)
    me = x * NC + c

    def zdev(off):
        return ((x * NZ + lax.rem(z + off + NZ, NZ)) * NC + c, y)

    def pdev(peer):
        return ((lax.div(peer, NC) * NZ + z) * NC + lax.rem(peer, NC), y)

    def peer_of(d):
        return lax.rem(me + d + PEERS, PEERS)

    def yof(d):
        return lax.rem(y + d + NY, NY)

    def ydev(d):
        return (ep, yof(d))

    counts = {"s": 0, "r": 0, "l": 0}
    pending = []

    def rsem_new():
        counts["r"] += 1
        return rsem.at[counts["r"] - 1]

    def send(src, dst, rs, dev):
        ss = ssem.at[counts["s"]]
        counts["s"] += 1
        cp = pltpu.make_async_remote_copy(
            src_ref=src, dst_ref=dst, send_sem=ss, recv_sem=rs, device_id=dev,
            device_id_type=pl.DeviceIdType.MESH,
        )
        cp.start()
        pending.append(cp)

    def recv(dst, rs):
        pltpu.make_async_remote_copy(
            src_ref=dst, dst_ref=dst, send_sem=rs, recv_sem=rs, device_id=(ep, y),
            device_id_type=pl.DeviceIdType.MESH,
        ).wait_recv()

    def local(src, dst):
        cp = pltpu.make_async_copy(src, dst, lsem.at[counts["l"]])
        counts["l"] += 1
        cp.start()
        return cp

    barrier = pltpu.get_barrier_semaphore()
    others = [zdev(1), zdev(-1)] + [pdev(peer_of(d)) for d in range(1, PEERS)] + [ydev(d) for d in range(1, NY)]
    for dev in others:
        pl.semaphore_signal(barrier, inc=1, device_id=dev, device_id_type=pl.DeviceIdType.MESH)
    mine = pl.ds(pl.multiple_of(y * DQ, DQ), DQ)
    cp_x = local(x_in.at[:, mine], XG.at[HOME])
    cp_m = local(meta_in, MG.at[HOME])
    cp_s = local(sw_in, SW.at[:, x, z, c])
    cp_sv = [local(saved.at[e, k], SVI.at[:, pl.ds((2 * e + k) * HQ, HQ)]) for e in range(NE) for k in range(2)]
    cp_w1 = local(down.at[:, :, mine], W1.at[:, pl.ds(pl.multiple_of(y * HQ, HQ), HQ), :])
    cp_w2 = local(gu.at[:, :, mine, :], W2.at[:, y])
    cp_xf = local(x_in, XF)
    pl.semaphore_wait(barrier, len(others))

    def slot(off):
        return (off + HOME) % NZ

    ag_sems = {}

    def ag_refs(s, direction, at_sender):
        hops = s - 1 if at_sender else s
        off = -hops if direction == 0 else hops
        k = slot(off)
        zz = lax.rem(z + off + NZ, NZ)
        if s < 8:
            return [XG.at[k], MG.at[k], SW.at[:, x, zz, c]]
        if direction == 0:
            return [XG.at[k, :, pl.ds(0, DQ // 2)], MG.at[k], SW.at[:, x, zz, c]]
        return [XG.at[k, :, pl.ds(DQ // 2, DQ // 2)]]

    def ag_send(s):
        for direction in range(2):
            srcs = ag_refs(s, direction, True)
            if s == 1:
                srcs = [x_in.at[:, mine], meta_in, sw_in]
            landing = ag_refs(s, direction, False)
            off_there = -s if direction == 0 else s
            dev = zdev(1 if direction == 0 else -1)
            for i, src in enumerate(srcs):
                rs = rsem_new()
                ag_sems[(s, direction, i)] = rs
                k = slot(off_there)
                zz = lax.rem(z + (-(s - 1) if direction == 0 else s - 1) + NZ, NZ)
                dst = [XG.at[k], MG.at[k], SW.at[:, x, zz, c]][i]
                if s == 8 and i == 0:
                    dst = XG.at[k, :, pl.ds(direction * (DQ // 2), DQ // 2)]
                send(src, dst, rs, dev)

    def ag_recv(s):
        for direction in range(2):
            for i, ref in enumerate(ag_refs(s, direction, False)):
                recv(ref, ag_sems[(s, direction, i)])

    ag_send(1)

    w1_sems, w2_sems = {}, {}
    for d in range(1, NY):
        w1_sems[d] = rsem_new()
        there = pl.ds(pl.multiple_of(yof(d) * DQ, DQ), DQ)
        send(down.at[:, :, there], W1.at[:, pl.ds(pl.multiple_of(y * HQ, HQ), HQ), :], w1_sems[d], ydev(d))
    for d in range(1, NY):
        w2_sems[d] = rsem_new()
        there = pl.ds(pl.multiple_of(yof(d) * DQ, DQ), DQ)
        send(gu.at[:, :, there, :], W2.at[:, y], w2_sems[d], ydev(d))

    for cp in cp_sv:
        cp.wait()

    def permute_saved(g):
        shape = (PEERS, SROWS, NZ * PEERS * CAP)
        src = lax.broadcasted_iota(jnp.int32, shape, 0)
        i = lax.broadcasted_iota(jnp.int32, shape, 1)
        lane = lax.broadcasted_iota(jnp.int32, shape, 2)
        j = lax.shift_right_logical(i * 43, 8)
        zz = (z + j + (SPAN * g - HOME + NZ)) & (NZ - 1)
        target = lax.shift_right_logical(src, 1) * (NZ * NC * CAP) + zz * (NC * CAP) + (src & 1) * CAP + (i - j * CAP)
        pick = jnp.where(target == lane, 1.0, 0.0).astype(BF).reshape(ROWS, NZ * PEERS * CAP)
        SVP[g] = dot_nn(pick, SVI[...]).astype(BF)

    qi = lax.broadcasted_iota(jnp.int32, (QN, TOK), 0)
    expert = (lax.shift_right_logical(qi, 2) * (NZ * NC * NE) + z * (NC * NE) + (qi & 3)).astype(F32)
    before = jnp.where(
        lax.broadcasted_iota(jnp.int32, (TOK, TOK), 0) < lax.broadcasted_iota(jnp.int32, (TOK, TOK), 1), 1.0, 0.0
    ).astype(BF)
    row3 = lax.broadcasted_iota(jnp.int32, (QN, SROWS, TOK), 1).astype(F32)
    lane_q = lax.broadcasted_iota(jnp.int32, (QN, QN * SROWS), 1)
    row_q = lax.broadcasted_iota(jnp.int32, (QN, QN * SROWS), 0)
    in_q = (lane_q >= row_q * SROWS) & (lane_q < row_q * SROWS + SROWS)
    spread = jnp.where(in_q, 1.0, 0.0).astype(BF)
    lane_i = jnp.sum(jnp.where(in_q, lane_q - row_q * SROWS, 0).astype(F32), axis=0, keepdims=True)

    def place(k):
        meta = MG[k]
        named = jnp.zeros((QN, TOK), F32)
        gate = jnp.zeros((QN, TOK), F32)
        for i in range(TOP):
            hit = meta[i:i + 1, :] == expert
            named = jnp.where(hit, 1.0, named)
            gate = jnp.where(hit, meta[TOP + i:TOP + i + 1, :], gate)
        rank = dot_nn(named.astype(BF), before)
        key = jnp.where(named > 0.5, rank + float((k % SPAN) * CAP), -1.0)
        return key, gate

    x_sems, b_sems = {}, {}

    def select(g):
        for j in range(SPAN):
            key, gate = place(g * SPAN + j)
            hot = jnp.where(key[:, None, :] == row3, 1.0, 0.0).astype(BF)
            SEL[:, pl.ds(j * TOK, TOK)] = hot.reshape(QN * SROWS, TOK)
        rows = XG[g * SPAN:(g + 1) * SPAN].reshape(SPAN * TOK, DQ)
        half = QN * SROWS // 2
        for h in range(2):
            got = dot_nn(SEL[pl.ds(h * half, half), :], rows).astype(BF)
            SB[g, h * (QN // 2):(h + 1) * (QN // 2)] = got.reshape(QN // 2, SROWS, DQ)
        for d in range(1, PEERS):
            rs = rsem_new()
            x_sems[(g, d)] = rs
            peer = peer_of(d)
            send(SB.at[g, pl.ds(peer * NE, NE)], R1.at[g, :, me], rs, pdev(peer))
        return local(SB.at[g, pl.ds(me * NE, NE)], R1.at[g, :, me])

    def weigh(g):
        for j in range(SPAN):
            key, gate = place(g * SPAN + j)
            high = gate.astype(BF)
            low = (gate - high.astype(F32)).astype(BF)
            where = dot_tn(key.astype(BF), spread) == lane_i
            at = pl.ds(j * TOK, TOK)
            WTH[g, at, :] = jnp.where(where, dot_tn(high, spread), 0.0).astype(BF)
            WTL[g, at, :] = jnp.where(where, dot_tn(low, spread), 0.0).astype(BF)

    keep = {}
    cp_x.wait()
    cp_m.wait()
    cp_s.wait()
    for s in range(1, 9):
        ag_recv(s)
        if s < 8:
            ag_send(s + 1)
        if s == 2:
            permute_saved(0)
        if s == 3:
            permute_saved(1)
        if s == 4:
            keep[0] = select(0)
        if s == 5:
            weigh(0)

    sw_sems = {}
    keep[1] = select(1)
    for d in range(1, PEERS):
        sw_sems[d] = rsem_new()
        peer = peer_of(d)
        part = SW.at[:, x, :, c]
        send(part, part, sw_sems[d], pdev(peer))

    h_sems, g_sems = {}, {}
    cp_w1.wait()
    for d in range(1, NY):
        src = yof(-d)
        recv(W1.at[:, pl.ds(pl.multiple_of(src * HQ, HQ), HQ), :], w1_sems[d])

    def hidden(g):
        keep[g].wait()
        for d in range(1, PEERS):
            recv(R1.at[g, :, peer_of(-d)], x_sems[(g, d)])
        for e in range(NE):
            rows = R1[g, e].reshape(ROWS, DQ)
            for d in list(range(1, NY)) + [0]:
                q = yof(d)
                part = dot_nt(rows, W1[e, pl.ds(pl.multiple_of(q * HQ, HQ), HQ), :])
                if d == 0:
                    HO[g, e] = part
                else:
                    HS[g, e, d - 1] = part.astype(BF)
                    rs = rsem_new()
                    h_sems[(g, e, d)] = rs
                    send(HS.at[g, e, d - 1], HR.at[g, e, d - 1], rs, ydev(d))

    def activate(g):
        for e in range(NE):
            h = HO[g, e]
            for d in range(1, NY):
                recv(HR.at[g, e, d - 1], h_sems[(g, e, d)])
                h = h + HR[g, e, d - 1].astype(F32)
            gate_pre = SVP[g, :, pl.ds(2 * e * HQ, HQ)]
            up_pre = SVP[g, :, pl.ds((2 * e + 1) * HQ, HQ)]
            a, b = act_grad(h, gate_pre, up_pre)
            G[g, e, y, 0] = a
            G[g, e, y, 1] = b
            for d in range(1, NY):
                rs = rsem_new()
                g_sems[(g, e, d)] = rs
                send(G.at[g, e, y], G.at[g, e, y], rs, ydev(d))

    def outward(g):
        for e in range(NE):
            for d in range(1, NY):
                recv(G.at[g, e, yof(-d)], g_sems[(g, e, d)])
            left = jnp.concatenate([G[g, e, q, k] for q in range(NY) for k in range(2)], axis=1)
            right = jnp.concatenate([W2[e, q, k] for q in range(NY) for k in range(2)], axis=1)
            OB[g, e] = dot_nt(left, right).astype(BF).reshape(PEERS, SROWS, DQ)
        for d in range(1, PEERS):
            rs = rsem_new()
            b_sems[(g, d)] = rs
            peer = peer_of(d)
            send(OB.at[g, :, peer], BK.at[g, pl.ds(me * NE, NE)], rs, pdev(peer))
        return local(OB.at[g, :, me], BK.at[g, pl.ds(me * NE, NE)])

    def combine(g):
        keep[g + 2].wait()
        for d in range(1, PEERS):
            recv(BK.at[g, pl.ds(peer_of(-d) * NE, NE)], b_sems[(g, d)])
        rows = BK[g].reshape(QN * SROWS, DQ)
        n = 4
        size = SPAN * TOK // n
        for i in range(n):
            at = pl.ds(i * size, size)
            got = dot_nn(WTH[g, at, :], rows) + dot_nn(WTL[g, at, :], rows)
            PT[g * SPAN + i * (SPAN // n):g * SPAN + (i + 1) * (SPAN // n)] = got.reshape(SPAN // n, TOK, DQ)

    s_sems = {}

    def shared():
        cp_xf.wait()
        for d in range(1, PEERS):
            peer = peer_of(-d)
            recv(SW.at[:, lax.div(peer, NC), :, lax.rem(peer, NC)], sw_sems[d])
        h = dot_nn(XF[...], SW[0].reshape(NX * DQ, HQ))
        a, b = act_grad(h, ssaved[0], ssaved[1])
        for d in list(range(1, NY)) + [0]:
            q = yof(d)
            part = dot_nt(a, SW[1, q].reshape(DQ, HQ)) + dot_nt(b, SW[2, q].reshape(DQ, HQ))
            if d == 0:
                SHO[...] = part
            else:
                SP[d - 1] = part
                s_sems[d] = rsem_new()
                send(SP.at[d - 1], SR.at[d - 1], s_sems[d], ydev(d))

    hidden(0)
    hidden(1)
    activate(1)
    activate(0)
    weigh(1)
    cp_w2.wait()
    for d in range(1, NY):
        recv(W2.at[:, yof(-d)], w2_sems[d])
    keep[3] = outward(1)
    keep[2] = outward(0)
    shared()

    z_sems = {}

    def rs_send(s):
        for direction in range(2):
            off = 9 - s if direction == 0 else s - 9
            cols = pl.ds(direction * (DQ // 2), DQ // 2)
            rs = rsem_new()
            z_sems[(s, direction)] = rs
            dev = zdev(1 if direction == 0 else -1)
            if s == 1:
                ZS[direction, s - 1, :, cols] = PT[slot(off), :, cols].astype(BF)
                send(ZS.at[direction, s - 1, :, cols], ZR.at[direction, s - 1, :, cols], rs, dev)
                continue
            if s == 2:
                recv(ZR.at[direction, 0, :, cols], z_sems[(1, direction)])
                other = pl.ds((1 - direction) * (DQ // 2), DQ // 2)
                ZS[direction, 1, :, cols] = (PT[slot(off), :, cols] + ZR[direction, 0, :, cols].astype(F32)).astype(BF)
                ZS[direction, 1, :, other] = PT[slot(off), :, other].astype(BF)
            else:
                recv(ZR.at[direction, s - 2], z_sems[(s - 1, direction)])
                ZS[direction, s - 1] = (PT[slot(off)] + ZR[direction, s - 2].astype(F32)).astype(BF)
            send(ZS.at[direction, s - 1], ZR.at[direction, s - 1], rs, dev)

    combine(1)
    rs_send(1)
    rs_send(2)
    combine(0)
    for s in range(3, 9):
        rs_send(s)
    total = PT[HOME] + SHO[...]
    for d in range(1, NY):
        recv(SR.at[d - 1], s_sems[d])
        total = total + SR[d - 1]
    for direction in range(2):
        recv(ZR.at[direction, 7], z_sems[(8, direction)])
        total = total + ZR[direction, 7].astype(F32)
    out[...] = total.astype(BF)
    for cp in pending:
        cp.wait_send()


def shards(
    grad_out, expert_ids, gate_values, saved_gate_up, expert_gate_up, expert_down,
    shared_saved, shared_gate_up, shared_down,
):
    meta = jnp.concatenate(
        [expert_ids.T.astype(F32), gate_values.T, jnp.zeros((24 - 2 * TOP, TOK), F32)], axis=0
    )
    sw = jnp.concatenate([shared_down.T[None], shared_gate_up], axis=0)
    anywhere = pl.BlockSpec(memory_space=pl.ANY)
    vmem = pl.BlockSpec(memory_space=pltpu.VMEM)
    slots = NZ * PEERS * CAP
    scratch = [
        pltpu.VMEM((NZ, TOK, DQ), BF),
        pltpu.VMEM((NZ, 24, TOK), F32),
        pltpu.VMEM((3, NX, NZ, NC, 16, HQ), BF),
        pltpu.VMEM((QN * SROWS, SPAN * TOK), BF),
        pltpu.VMEM((GROUPS, SPAN * TOK, QN * SROWS), BF),
        pltpu.VMEM((GROUPS, SPAN * TOK, QN * SROWS), BF),
        pltpu.VMEM((GROUPS, QN, SROWS, DQ), BF),
        pltpu.VMEM((GROUPS, NE, PEERS, SROWS, DQ), BF),
        pltpu.VMEM((NE, NY * HQ, DQ), BF),
        pltpu.VMEM((NE, NY, 2, DQ, HQ), BF),
        pltpu.VMEM((slots, 2 * NE * HQ), BF),
        pltpu.VMEM((GROUPS, ROWS, 2 * NE * HQ), BF),
        pltpu.VMEM((GROUPS, NE, ROWS, HQ), F32),
        pltpu.VMEM((GROUPS, NE, NY - 1, ROWS, HQ), BF),
        pltpu.VMEM((GROUPS, NE, NY - 1, ROWS, HQ), BF),
        pltpu.VMEM((GROUPS, NE, NY, 2, ROWS, HQ), BF),
        pltpu.VMEM((GROUPS, NE, PEERS, SROWS, DQ), BF),
        pltpu.VMEM((GROUPS, QN, SROWS, DQ), BF),
        pltpu.VMEM((NZ, TOK, DQ), F32),
        pltpu.VMEM((2, 8, TOK, DQ), BF),
        pltpu.VMEM((2, 8, TOK, DQ), BF),
        pltpu.VMEM((TOK, NX * DQ), BF),
        pltpu.VMEM((TOK, DQ), F32),
        pltpu.VMEM((NY - 1, TOK, DQ), F32),
        pltpu.VMEM((NY - 1, TOK, DQ), F32),
        pltpu.SemaphoreType.DMA((136,)),
        pltpu.SemaphoreType.DMA((136,)),
        pltpu.SemaphoreType.DMA((16,)),
    ]
    return pl.pallas_call(
        kernel,
        out_shape=jax.ShapeDtypeStruct((TOK, DQ), BF),
        in_specs=[anywhere] * 6 + [vmem],
        out_specs=vmem,
        scratch_shapes=scratch,
        compiler_params=pltpu.CompilerParams(
            collective_id=0, has_side_effects=True, vmem_limit_bytes=60 * 1024 * 1024
        ),
        cost_estimate=pl.CostEstimate(flops=8_000_000_000, bytes_accessed=8_000_000, transcendentals=400_000),
    )(grad_out, meta, sw, saved_gate_up, expert_gate_up, expert_down, shared_saved)


def solution(mesh):
    in_specs = (
        P("ep", None),
        P("ep", None),
        P("ep", None),
        P("ep", None, None, "tp"),
        P("ep", None, None, "tp"),
        P("ep", "tp", None),
        P(None, "ep", "tp"),
        P(None, "ep", "tp"),
        P("tp", "ep"),
    )
    return jax.shard_map(shards, mesh=mesh, in_specs=in_specs, out_specs=P("ep", "tp"), check_vma=False)
```

time: 864 us -> 163 us (0.19)
  blocking collectives: 350 us -> 0 us
  waiting for transfers between devices: 302 us -> 0 us
  Pallas kernels: 0 us -> 156 us
  local copies, waits for them, and re-layouts: 121 us -> 1.65 us
  starting transfers between devices: 34.4 us -> 0 us
  other arithmetic: 21.5 us -> 3.37 us
  matrix products: 18 us -> 0 us
  between operations: 14.1 us -> 0.01 us
    all_gather x1 -> x0, blocking collectives: 350 us -> none  [shards(): lax.all_gather(shared_down, 'ep', axis=1, tiled=True)]
    all_to_all x2 -> x0, waiting for transfers between devices: 273 us -> none  [the longest x1 273 us: shards(): lax.all_to_all(outgoing, 'ep', split_axis=0, concat_axis=0, tiled=True)]
    pallas_call x0 -> x1, Pallas kernels: none -> 156 us  [shards(): pl.pallas_call(kernel, out_shape=jax.ShapeDtypeStruct((TOK, DQ), BF), in_...]
    all_to_all x2 -> x0, starting transfers between devices: 34.3 us -> none  [the longest x1 20.9 us: shards(): lax.all_to_all(outgoing, 'ep', split_axis=0, concat_axis=0, tiled=True)]
    gather x3 -> x0, local copies, waits for them, and re-layouts: 32.4 us -> none  [the longest x2 18 us: shards(): grad_out[owner_token]]
    reduce_scatter x1 -> x0, waiting for transfers between devices: 27.8 us -> none  [shards(): lax.psum_scatter(routed + shared_part, 'tp', scatter_dimension=1, tiled=T...]
    scatter x2 -> x0, local copies, waits for them, and re-layouts: 27.5 us -> none  [the longest x1 22.2 us: shards(): jnp.zeros((all_experts * capacity,), jnp.bool_).at[slot_index].set(True)]
    convert_element_type x4 -> x0, local copies, waits for them, and re-layouts: 24.3 us -> none  [the longest x1 12.7 us: shards(): going_back = partial_value.astype(jnp.bfloat16)]
  transfers between devices with their start and end apart: 4 -> 0, of which waited for: 2 -> 0; matrix products, arithmetic and copies ran while one was open for 0% -> 0% of each run, Pallas kernels for 0% -> 0%
where the time goes in v1:
time: 163 us; the launch traced here: 161 us
  Pallas kernels  156 us (96%)
  other arithmetic  3.37 us (2%)
  local copies, waits for them, and re-layouts  1.65 us (1%)
    pallas_call x1, Pallas kernels, shards(): pl.pallas_call(kernel, out_shape=jax.ShapeDtypeStruct((TOK, DQ), BF), in_...  156 us

profile of v1, /device:TPU:1, one launch (start us, length us, event | category | flops | bytes accessed | tf_op | source)
XLA Modules:
  0.0 161.0 jit_solution(16739691002820773471)
XLA Ops:
  0.0 0.1 pad.4.clone
  0.1 0.7 convert_bitcast_fusion
  0.8 1.4 maximum_maximum_fusion.meta_in
  2.1 1.3 pad_maximum_fusion.sw_in
  3.4 155.9 %shard_map.91 = bf16[128,512]{1,0:T(8,128)(2,1)} custom-call(bf16[128,2048]{1,0:T(8,128)(2,1)} %x_in.1, f32[24,128]{1,0:T(8,128)} %maximum_maximum_fusion.meta_in, bf16[3,16,128]{2,1,0:T(8,128)(2,1)} %pad_maximum_fusion.sw_in, bf16[2,2,768,128]{3,2,1,0:T(8,128)(2,1)} %saved.1, bf16[2,2,2048,128]{3,2,1,0:T(8,128)(2,1)} %gu.1, bf16[2,128,2048]{2,1,0:T(8,128)(2,1)} %down.1, ...), custom_call_target="tpu_custom_call" | custom-call | flops 8000000000 | bytes 8000000 | tf_op jit(solution)/shard_map/pallas_call | solution.py:438
  159.4 1.6 copy.11
  (1 shorter events, 0.0 us)

commit v2 on v1

--- a/solution.py
+++ b/solution.py
@@ -23,6 +23,10 @@
 QN = PEERS * NE
 ROWS = PEERS * SROWS
 HOME = 3
+AGC = 4
+AGR = TOK // AGC
+RSC = 4
+RSR = TOK // RSC
 
 
 def dot_nt(a, b):
@@ -45,7 +49,7 @@
 
 
 def kernel(
-    x_in, meta_in, sw_in, saved, gu, down, ssaved, out,
+    x_in, ids, gates, sd, sgu, saved, gu, down, ssaved, out,
     XG, MG, SW, SEL, WTH, WTL, SB, R1, W1, W2, SVI, SVP, HO, HS, HR, G, OB, BK, PT, ZS, ZR, XF, SHO, SP, SR,
     ssem, rsem, lsem,
 ):
@@ -106,8 +110,7 @@
         pl.semaphore_signal(barrier, inc=1, device_id=dev, device_id_type=pl.DeviceIdType.MESH)
     mine = pl.ds(pl.multiple_of(y * DQ, DQ), DQ)
     cp_x = local(x_in.at[:, mine], XG.at[HOME])
-    cp_m = local(meta_in, MG.at[HOME])
-    cp_s = local(sw_in, SW.at[:, x, z, c])
+    cp_s = local(sgu, SW.at[pl.ds(1, 2), x, z, c])
     cp_sv = [local(saved.at[e, k], SVI.at[:, pl.ds((2 * e + k) * HQ, HQ)]) for e in range(NE) for k in range(2)]
     cp_w1 = local(down.at[:, :, mine], W1.at[:, pl.ds(pl.multiple_of(y * HQ, HQ), HQ), :])
     cp_w2 = local(gu.at[:, :, mine, :], W2.at[:, y])
@@ -118,42 +121,51 @@
         return (off + HOME) % NZ
 
     ag_sems = {}
-
-    def ag_refs(s, direction, at_sender):
-        hops = s - 1 if at_sender else s
-        off = -hops if direction == 0 else hops
+    SWI = AGC + 1
+
+    def ag_ref(s, direction, i):
+        off = -s if direction == 0 else s
         k = slot(off)
-        zz = lax.rem(z + off + NZ, NZ)
-        if s < 8:
-            return [XG.at[k], MG.at[k], SW.at[:, x, zz, c]]
-        if direction == 0:
-            return [XG.at[k, :, pl.ds(0, DQ // 2)], MG.at[k], SW.at[:, x, zz, c]]
-        return [XG.at[k, :, pl.ds(DQ // 2, DQ // 2)]]
-
-    def ag_send(s):
+        if s == 8 and (i in (0, SWI) or 1 <= i <= AGC // 2) != (direction == 0):
+            return None
+        if i == 0:
+            return MG.at[k]
+        if i == SWI:
+            return SW.at[:, x, lax.rem(z + off + NZ, NZ), c]
+        return XG.at[k, pl.ds((i - 1) * AGR, AGR), :]
+
+    def ag_send(s, direction, i):
+        there = ag_ref(s, direction, i)
+        if there is None:
+            return
+        off = -s if direction == 0 else s
+        k = slot(off)
+        src = ag_ref(s - 1, direction, i) if s < 9 else None
+        if i == 0:
+            dst = MG.at[k]
+        elif i == SWI:
+            dst = src
+        else:
+            dst = XG.at[k, pl.ds((i - 1) * AGR, AGR), :]
+            if s == 1:
+                src = x_in.at[pl.ds((i - 1) * AGR, AGR), mine]
+        rs = rsem_new()
+        ag_sems[(s, direction, i)] = rs
+        send(src, dst, rs, zdev(1 if direction == 0 else -1))
+
+    for i in range(1, AGC + 1):
         for direction in range(2):
-            srcs = ag_refs(s, direction, True)
-            if s == 1:
-                srcs = [x_in.at[:, mine], meta_in, sw_in]
-            landing = ag_refs(s, direction, False)
-            off_there = -s if direction == 0 else s
-            dev = zdev(1 if direction == 0 else -1)
-            for i, src in enumerate(srcs):
-                rs = rsem_new()
-                ag_sems[(s, direction, i)] = rs
-                k = slot(off_there)
-                zz = lax.rem(z + (-(s - 1) if direction == 0 else s - 1) + NZ, NZ)
-                dst = [XG.at[k], MG.at[k], SW.at[:, x, zz, c]][i]
-                if s == 8 and i == 0:
-                    dst = XG.at[k, :, pl.ds(direction * (DQ // 2), DQ // 2)]
-                send(src, dst, rs, dev)
-
-    def ag_recv(s):
-        for direction in range(2):
-            for i, ref in enumerate(ag_refs(s, direction, False)):
-                recv(ref, ag_sems[(s, direction, i)])
-
-    ag_send(1)
+            ag_send(1, direction, i)
+
+    MG[HOME, 0:TOP] = ids[...].astype(F32)
+    MG[HOME, TOP:2 * TOP] = gates[...]
+    MG[HOME, 2 * TOP:24] = jnp.zeros((24 - 2 * TOP, TOK), F32)
+    SW[0, x, z, c] = sd[...]
+    for direction in range(2):
+        ag_send(1, direction, 0)
+    cp_s.wait()
+    for direction in range(2):
+        ag_send(1, direction, SWI)
 
     w1_sems, w2_sems = {}, {}
     for d in range(1, NY):
@@ -234,15 +246,18 @@
 
     keep = {}
     cp_x.wait()
-    cp_m.wait()
-    cp_s.wait()
     for s in range(1, 9):
-        ag_recv(s)
-        if s < 8:
-            ag_send(s + 1)
+        for i in range(AGC + 2):
+            for direction in range(2):
+                ref = ag_ref(s, direction, i)
+                if ref is None:
+                    continue
+                recv(ref, ag_sems[(s, direction, i)])
+                if s < 8:
+                    ag_send(s + 1, direction, i)
+        if s == 1:
+            permute_saved(0)
         if s == 2:
-            permute_saved(0)
-        if s == 3:
             permute_saved(1)
         if s == 4:
             keep[0] = select(0)
@@ -251,11 +266,12 @@
 
     sw_sems = {}
     keep[1] = select(1)
-    for d in range(1, PEERS):
-        sw_sems[d] = rsem_new()
-        peer = peer_of(d)
-        part = SW.at[:, x, :, c]
-        send(part, part, sw_sems[d], pdev(peer))
+
+    def spread_shared():
+        for d in range(1, PEERS):
+            sw_sems[d] = rsem_new()
+            part = SW.at[:, x, :, c]
+            send(part, part, sw_sems[d], pdev(peer_of(d)))
 
     h_sems, g_sems = {}, {}
     cp_w1.wait()
@@ -280,26 +296,33 @@
                     h_sems[(g, e, d)] = rs
                     send(HS.at[g, e, d - 1], HR.at[g, e, d - 1], rs, ydev(d))
 
-    def activate(g):
-        for e in range(NE):
-            h = HO[g, e]
-            for d in range(1, NY):
-                recv(HR.at[g, e, d - 1], h_sems[(g, e, d)])
-                h = h + HR[g, e, d - 1].astype(F32)
-            gate_pre = SVP[g, :, pl.ds(2 * e * HQ, HQ)]
-            up_pre = SVP[g, :, pl.ds((2 * e + 1) * HQ, HQ)]
-            a, b = act_grad(h, gate_pre, up_pre)
-            G[g, e, y, 0] = a
-            G[g, e, y, 1] = b
-            for d in range(1, NY):
-                rs = rsem_new()
-                g_sems[(g, e, d)] = rs
-                send(G.at[g, e, y], G.at[g, e, y], rs, ydev(d))
+    def activate(g, e):
+        h = HO[g, e]
+        for d in range(1, NY):
+            recv(HR.at[g, e, d - 1], h_sems[(g, e, d)])
+            h = h + HR[g, e, d - 1].astype(F32)
+        gate_pre = SVP[g, :, pl.ds(2 * e * HQ, HQ)]
+        up_pre = SVP[g, :, pl.ds((2 * e + 1) * HQ, HQ)]
+        a, b = act_grad(h, gate_pre, up_pre)
+        G[g, e, y, 0] = a
+        G[g, e, y, 1] = b
+        for d in (1, -1):
+            rs = rsem_new()
+            g_sems[(g, e, d)] = rs
+            send(G.at[g, e, y], G.at[g, e, y], rs, ydev(d))
+
+    def relay(g, e):
+        for k, d in ((0, 1), (1, -1)):
+            piece = G.at[g, e, yof(-d)]
+            recv(piece, g_sems[(g, e, d)])
+            rs = rsem_new()
+            g_sems[(g, e, 2, k)] = rs
+            send(piece.at[k], piece.at[k], rs, ydev(d))
 
     def outward(g):
         for e in range(NE):
-            for d in range(1, NY):
-                recv(G.at[g, e, yof(-d)], g_sems[(g, e, d)])
+            for k in range(2):
+                recv(G.at[g, e, yof(2), k], g_sems[(g, e, 2, k)])
             left = jnp.concatenate([G[g, e, q, k] for q in range(NY) for k in range(2)], axis=1)
             right = jnp.concatenate([W2[e, q, k] for q in range(NY) for k in range(2)], axis=1)
             OB[g, e] = dot_nt(left, right).astype(BF).reshape(PEERS, SROWS, DQ)
@@ -324,7 +347,7 @@
 
     s_sems = {}
 
-    def shared():
+    def shared_products():
         cp_xf.wait()
         for d in range(1, PEERS):
             peer = peer_of(-d)
@@ -338,58 +361,72 @@
                 SHO[...] = part
             else:
                 SP[d - 1] = part
-                s_sems[d] = rsem_new()
-                send(SP.at[d - 1], SR.at[d - 1], s_sems[d], ydev(d))
+
+    def shared_sum():
+        for d in range(1, NY):
+            s_sems[d] = rsem_new()
+            send(SP.at[d - 1], SR.at[d - 1], s_sems[d], ydev(d))
 
     hidden(0)
+    weigh(1)
+    activate(0, 0)
     hidden(1)
-    activate(1)
-    activate(0)
-    weigh(1)
+    spread_shared()
+    activate(1, 0)
+    activate(1, 1)
+    relay(0, 0)
+    activate(0, 1)
+    relay(1, 0)
+    relay(1, 1)
     cp_w2.wait()
     for d in range(1, NY):
         recv(W2.at[:, yof(-d)], w2_sems[d])
     keep[3] = outward(1)
+    relay(0, 1)
+    shared_products()
     keep[2] = outward(0)
-    shared()
+    shared_sum()
 
     z_sems = {}
 
-    def rs_send(s):
-        for direction in range(2):
-            off = 9 - s if direction == 0 else s - 9
-            cols = pl.ds(direction * (DQ // 2), DQ // 2)
-            rs = rsem_new()
-            z_sems[(s, direction)] = rs
-            dev = zdev(1 if direction == 0 else -1)
-            if s == 1:
-                ZS[direction, s - 1, :, cols] = PT[slot(off), :, cols].astype(BF)
-                send(ZS.at[direction, s - 1, :, cols], ZR.at[direction, s - 1, :, cols], rs, dev)
-                continue
-            if s == 2:
-                recv(ZR.at[direction, 0, :, cols], z_sems[(1, direction)])
-                other = pl.ds((1 - direction) * (DQ // 2), DQ // 2)
-                ZS[direction, 1, :, cols] = (PT[slot(off), :, cols] + ZR[direction, 0, :, cols].astype(F32)).astype(BF)
-                ZS[direction, 1, :, other] = PT[slot(off), :, other].astype(BF)
-            else:
-                recv(ZR.at[direction, s - 2], z_sems[(s - 1, direction)])
-                ZS[direction, s - 1] = (PT[slot(off)] + ZR[direction, s - 2].astype(F32)).astype(BF)
-            send(ZS.at[direction, s - 1], ZR.at[direction, s - 1], rs, dev)
+    def rs_step(s):
+        for i in range(RSC):
+            rows = pl.ds(i * RSR, RSR)
+            for direction in range(2):
+                if s == 1 and (i < RSC // 2) != (direction == 0):
+                    continue
+                off = 9 - s if direction == 0 else s - 9
+                part = PT[slot(off), rows, :]
+                if (s - 1, direction, i) in z_sems:
+                    recv(ZR.at[direction, s - 2, rows, :], z_sems[(s - 1, direction, i)])
+                    part = part + ZR[direction, s - 2, rows, :].astype(F32)
+                ZS[direction, s - 1, rows, :] = part.astype(BF)
+                rs = rsem_new()
+                z_sems[(s, direction, i)] = rs
+                send(
+                    ZS.at[direction, s - 1, rows, :], ZR.at[direction, s - 1, rows, :], rs,
+                    zdev(1 if direction == 0 else -1),
+                )
 
     combine(1)
-    rs_send(1)
-    rs_send(2)
+    rs_step(1)
+    rs_step(2)
+    rs_step(3)
     combine(0)
-    for s in range(3, 9):
-        rs_send(s)
+    for s in range(4, 9):
+        rs_step(s)
     total = PT[HOME] + SHO[...]
     for d in range(1, NY):
         recv(SR.at[d - 1], s_sems[d])
         total = total + SR[d - 1]
-    for direction in range(2):
-        recv(ZR.at[direction, 7], z_sems[(8, direction)])
-        total = total + ZR[direction, 7].astype(F32)
-    out[...] = total.astype(BF)
+    PT[HOME] = total
+    for i in range(RSC):
+        rows = pl.ds(i * RSR, RSR)
+        part = PT[HOME, rows, :]
+        for direction in range(2):
+            recv(ZR.at[direction, 7, rows, :], z_sems[(8, direction, i)])
+            part = part + ZR[direction, 7, rows, :].astype(F32)
+        out[rows, :] = part.astype(BF)
     for cp in pending:
         cp.wait_send()
 
@@ -398,10 +435,6 @@
     grad_out, expert_ids, gate_values, saved_gate_up, expert_gate_up, expert_down,
     shared_saved, shared_gate_up, shared_down,
 ):
-    meta = jnp.concatenate(
-        [expert_ids.T.astype(F32), gate_values.T, jnp.zeros((24 - 2 * TOP, TOK), F32)], axis=0
-    )
-    sw = jnp.concatenate([shared_down.T[None], shared_gate_up], axis=0)
     anywhere = pl.BlockSpec(memory_space=pl.ANY)
     vmem = pl.BlockSpec(memory_space=pltpu.VMEM)
     slots = NZ * PEERS * CAP
@@ -431,21 +464,24 @@
         pltpu.VMEM((TOK, DQ), F32),
         pltpu.VMEM((NY - 1, TOK, DQ), F32),
         pltpu.VMEM((NY - 1, TOK, DQ), F32),
-        pltpu.SemaphoreType.DMA((136,)),
-        pltpu.SemaphoreType.DMA((136,)),
+        pltpu.SemaphoreType.DMA((228,)),
+        pltpu.SemaphoreType.DMA((228,)),
         pltpu.SemaphoreType.DMA((16,)),
     ]
     return pl.pallas_call(
         kernel,
         out_shape=jax.ShapeDtypeStruct((TOK, DQ), BF),
-        in_specs=[anywhere] * 6 + [vmem],
+        in_specs=[anywhere, vmem, vmem, vmem, anywhere, anywhere, anywhere, anywhere, vmem],
         out_specs=vmem,
         scratch_shapes=scratch,
         compiler_params=pltpu.CompilerParams(
             collective_id=0, has_side_effects=True, vmem_limit_bytes=60 * 1024 * 1024
         ),
         cost_estimate=pl.CostEstimate(flops=8_000_000_000, bytes_accessed=8_000_000, transcendentals=400_000),
-    )(grad_out, meta, sw, saved_gate_up, expert_gate_up, expert_down, shared_saved)
+    )(
+        grad_out, expert_ids.T, gate_values.T, shared_down.T, shared_gate_up, saved_gate_up, expert_gate_up, expert_down,
+        shared_saved,
+    )
 
 
 def solution(mesh):

time: 163 us -> 138 us (0.85)
  Pallas kernels: 156 us -> 135 us
  other arithmetic: 3.37 us -> 0 us
    pallas_call x1, Pallas kernels: 156 us -> 135 us  [shards(): pl.pallas_call(kernel, out_shape=jax.ShapeDtypeStruct((TOK, DQ), BF), in_...]
    concatenate x2 -> x0, other arithmetic: 2.67 us -> none  [the longest x1 1.37 us: shards(): jnp.concatenate([expert_ids.T.astype(F32), gate_values.T, jnp.zeros((24 -...]
where the time goes in v2:
time: 138 us; the launch traced here: 137 us
  Pallas kernels  135 us (98%)
  local copies, waits for them, and re-layouts  1.57 us (1%)
    pallas_call x1, Pallas kernels, shards(): pl.pallas_call(kernel, out_shape=jax.ShapeDtypeStruct((TOK, DQ), BF), in_...  135 us

profile of v2, /device:TPU:1, one launch (start us, length us, event | category | flops | bytes accessed | tf_op | source)
XLA Modules:
  0.0 136.8 jit_solution(16289905096638404940)
XLA Ops:
  0.0 135.2 %shard_map.91 = bf16[128,512]{1,0:T(8,128)(2,1)} custom-call(bf16[128,2048]{1,0:T(8,128)(2,1)} %x_in.1, s32[10,128]{1,0:T(8,128)} %bitcast.3, f32[10,128]{1,0:T(8,128)} %bitcast.4, bf16[16,128]{1,0:T(8,128)(2,1)} %bitcast.5, bf16[2,16,128]{2,1,0:T(8,128)(2,1)} %sgu.1, bf16[2,2,768,128]{3,2,1,0:T(8,128)(2,1)} %saved.1, bf16[2,2,2048,128]{3,2,1,0:T(8,128)(2,1)} %gu.1, ...), custom_call_target="tpu_custom_call" | custom-call | flops 8000000000 | bytes 8000000 | tf_op jit(solution)/shard_map/pallas_call | solution.py:471
  135.2 1.6 %copy.11 = bf16[128,512]{1,0:T(8,128)(2,1)} copy(bf16[128,512]{1,0:T(8,128)(2,1)} %shard_map.91) | data formatting | bytes 262144

commit v3 on v2

--- a/solution.py
+++ b/solution.py
@@ -17,16 +17,18 @@
 DQ = 512
 HQ = 128
 NE = 2
-GROUPS = 2
+GROUPS = 4
 SPAN = NZ // GROUPS
 SROWS = SPAN * CAP
 QN = PEERS * NE
-ROWS = PEERS * SROWS
-HOME = 3
+PR = NE * SROWS
+ROWS = PEERS * PR
+HOME = 0
 AGC = 4
 AGR = TOK // AGC
 RSC = 4
 RSR = TOK // RSC
+OFFS = (0, 1, -1, 2, -2, 3, -3, 4, -4, 5, -5, 6, -6, 7, -7, 8)
 
 
 def dot_nt(a, b):
@@ -118,7 +120,7 @@
     pl.semaphore_wait(barrier, len(others))
 
     def slot(off):
-        return (off + HOME) % NZ
+        return OFFS.index(8 if off == -8 else off)
 
     ag_sems = {}
     SWI = AGC + 1
@@ -153,43 +155,54 @@
         ag_sems[(s, direction, i)] = rs
         send(src, dst, rs, zdev(1 if direction == 0 else -1))
 
-    for i in range(1, AGC + 1):
-        for direction in range(2):
-            ag_send(1, direction, i)
-
     MG[HOME, 0:TOP] = ids[...].astype(F32)
     MG[HOME, TOP:2 * TOP] = gates[...]
     MG[HOME, 2 * TOP:24] = jnp.zeros((24 - 2 * TOP, TOK), F32)
     SW[0, x, z, c] = sd[...]
+    w1_sems, w2_sems = {}, {}
+
+    def send_w1():
+        for d in range(1, NY):
+            w1_sems[d] = rsem_new()
+            there = pl.ds(pl.multiple_of(yof(d) * DQ, DQ), DQ)
+            send(down.at[:, :, there], W1.at[:, pl.ds(pl.multiple_of(y * HQ, HQ), HQ), :], w1_sems[d], ydev(d))
+
+    def send_w2():
+        for d in range(1, NY):
+            w2_sems[d] = rsem_new()
+            there = pl.ds(pl.multiple_of(yof(d) * DQ, DQ), DQ)
+            send(gu.at[:, :, there, :], W2.at[:, y], w2_sems[d], ydev(d))
+
     for direction in range(2):
         ag_send(1, direction, 0)
+    send_w1()
+    for i in range(1, AGC + 1):
+        for direction in range(2):
+            ag_send(1, direction, i)
     cp_s.wait()
     for direction in range(2):
         ag_send(1, direction, SWI)
 
-    w1_sems, w2_sems = {}, {}
-    for d in range(1, NY):
-        w1_sems[d] = rsem_new()
-        there = pl.ds(pl.multiple_of(yof(d) * DQ, DQ), DQ)
-        send(down.at[:, :, there], W1.at[:, pl.ds(pl.multiple_of(y * HQ, HQ), HQ), :], w1_sems[d], ydev(d))
-    for d in range(1, NY):
-        w2_sems[d] = rsem_new()
-        there = pl.ds(pl.multiple_of(yof(d) * DQ, DQ), DQ)
-        send(gu.at[:, :, there, :], W2.at[:, y], w2_sems[d], ydev(d))
-
     for cp in cp_sv:
         cp.wait()
 
+    def second(width):
+        return lax.broadcasted_iota(jnp.int32, (PEERS, PR, width), 1).reshape(ROWS, width) >= SROWS
+
     def permute_saved(g):
-        shape = (PEERS, SROWS, NZ * PEERS * CAP)
+        shape = (PEERS, PR, NZ * PEERS * CAP)
         src = lax.broadcasted_iota(jnp.int32, shape, 0)
         i = lax.broadcasted_iota(jnp.int32, shape, 1)
         lane = lax.broadcasted_iota(jnp.int32, shape, 2)
+        i = jnp.where(i >= SROWS, i - SROWS, i)
         j = lax.shift_right_logical(i * 43, 8)
-        zz = (z + j + (SPAN * g - HOME + NZ)) & (NZ - 1)
+        offs = [(o + NZ) % NZ for o in OFFS[g * SPAN:(g + 1) * SPAN]]
+        off = jnp.where(j == 0, offs[0], jnp.where(j == 1, offs[1], jnp.where(j == 2, offs[2], offs[3])))
+        zz = (z + off) & (NZ - 1)
         target = lax.shift_right_logical(src, 1) * (NZ * NC * CAP) + zz * (NC * CAP) + (src & 1) * CAP + (i - j * CAP)
         pick = jnp.where(target == lane, 1.0, 0.0).astype(BF).reshape(ROWS, NZ * PEERS * CAP)
-        SVP[g] = dot_nn(pick, SVI[...]).astype(BF)
+        got = dot_nn(pick, SVI[...])
+        SVP[g] = jnp.where(second(2 * HQ), got[:, 2 * HQ:], got[:, :2 * HQ]).astype(BF)
 
     qi = lax.broadcasted_iota(jnp.int32, (QN, TOK), 0)
     expert = (lax.shift_right_logical(qi, 2) * (NZ * NC * NE) + z * (NC * NE) + (qi & 3)).astype(F32)
@@ -220,19 +233,16 @@
     def select(g):
         for j in range(SPAN):
             key, gate = place(g * SPAN + j)
-            hot = jnp.where(key[:, None, :] == row3, 1.0, 0.0).astype(BF)
-            SEL[:, pl.ds(j * TOK, TOK)] = hot.reshape(QN * SROWS, TOK)
+            hot = jnp.where(key[:, None, :] == row3, 1.0, 0.0).reshape(QN * SROWS, TOK)
+            SEL[:, pl.ds(j * TOK, TOK)] = hot.astype(BF)
         rows = XG[g * SPAN:(g + 1) * SPAN].reshape(SPAN * TOK, DQ)
-        half = QN * SROWS // 2
-        for h in range(2):
-            got = dot_nn(SEL[pl.ds(h * half, half), :], rows).astype(BF)
-            SB[g, h * (QN // 2):(h + 1) * (QN // 2)] = got.reshape(QN // 2, SROWS, DQ)
+        SB[g] = dot_nn(SEL[...], rows).astype(BF).reshape(PEERS, PR, DQ)
         for d in range(1, PEERS):
             rs = rsem_new()
             x_sems[(g, d)] = rs
             peer = peer_of(d)
-            send(SB.at[g, pl.ds(peer * NE, NE)], R1.at[g, :, me], rs, pdev(peer))
-        return local(SB.at[g, pl.ds(me * NE, NE)], R1.at[g, :, me])
+            send(SB.at[g, peer], R1.at[g, me], rs, pdev(peer))
+        return local(SB.at[g, me], R1.at[g, me])
 
     def weigh(g):
         for j in range(SPAN):
@@ -244,28 +254,7 @@
             WTH[g, at, :] = jnp.where(where, dot_tn(high, spread), 0.0).astype(BF)
             WTL[g, at, :] = jnp.where(where, dot_tn(low, spread), 0.0).astype(BF)
 
-    keep = {}
-    cp_x.wait()
-    for s in range(1, 9):
-        for i in range(AGC + 2):
-            for direction in range(2):
-                ref = ag_ref(s, direction, i)
-                if ref is None:
-                    continue
-                recv(ref, ag_sems[(s, direction, i)])
-                if s < 8:
-                    ag_send(s + 1, direction, i)
-        if s == 1:
-            permute_saved(0)
-        if s == 2:
-            permute_saved(1)
-        if s == 4:
-            keep[0] = select(0)
-        if s == 5:
-            weigh(0)
-
-    sw_sems = {}
-    keep[1] = select(1)
+    keep, sw_sems, h_sems, g_sems = {}, {}, {}, {}
 
     def spread_shared():
         for d in range(1, PEERS):
@@ -273,77 +262,78 @@
             part = SW.at[:, x, :, c]
             send(part, part, sw_sems[d], pdev(peer_of(d)))
 
-    h_sems, g_sems = {}, {}
-    cp_w1.wait()
-    for d in range(1, NY):
-        src = yof(-d)
-        recv(W1.at[:, pl.ds(pl.multiple_of(src * HQ, HQ), HQ), :], w1_sems[d])
+    def wait_w1():
+        cp_w1.wait()
+        for d in range(1, NY):
+            recv(W1.at[:, pl.ds(pl.multiple_of(yof(-d) * HQ, HQ), HQ), :], w1_sems[d])
+
+    def wait_w2():
+        cp_w2.wait()
+        for d in range(1, NY):
+            recv(W2.at[:, yof(-d)], w2_sems[d])
 
     def hidden(g):
         keep[g].wait()
         for d in range(1, PEERS):
-            recv(R1.at[g, :, peer_of(-d)], x_sems[(g, d)])
-        for e in range(NE):
-            rows = R1[g, e].reshape(ROWS, DQ)
-            for d in list(range(1, NY)) + [0]:
-                q = yof(d)
-                part = dot_nt(rows, W1[e, pl.ds(pl.multiple_of(q * HQ, HQ), HQ), :])
-                if d == 0:
-                    HO[g, e] = part
-                else:
-                    HS[g, e, d - 1] = part.astype(BF)
-                    rs = rsem_new()
-                    h_sems[(g, e, d)] = rs
-                    send(HS.at[g, e, d - 1], HR.at[g, e, d - 1], rs, ydev(d))
-
-    def activate(g, e):
-        h = HO[g, e]
+            recv(R1.at[g, peer_of(-d)], x_sems[(g, d)])
+        rows = R1[g].reshape(ROWS, DQ)
+        mine_second = second(HQ)
+        for d in (1, 2, 3, 0):
+            quarter = pl.ds(pl.multiple_of(yof(d) * HQ, HQ), HQ)
+            both = dot_nt(rows, jnp.concatenate([W1[e, quarter, :] for e in range(NE)], axis=0))
+            part = jnp.where(mine_second, both[:, HQ:], both[:, :HQ])
+            if d == 0:
+                HO[g] = part
+            else:
+                HS[g, d - 1] = part.astype(BF)
+                rs = rsem_new()
+                h_sems[(g, d)] = rs
+                send(HS.at[g, d - 1], HR.at[g, d - 1], rs, ydev(d))
+
+    def activate(g):
+        h = HO[g]
         for d in range(1, NY):
-            recv(HR.at[g, e, d - 1], h_sems[(g, e, d)])
-            h = h + HR[g, e, d - 1].astype(F32)
-        gate_pre = SVP[g, :, pl.ds(2 * e * HQ, HQ)]
-        up_pre = SVP[g, :, pl.ds((2 * e + 1) * HQ, HQ)]
-        a, b = act_grad(h, gate_pre, up_pre)
-        G[g, e, y, 0] = a
-        G[g, e, y, 1] = b
+            recv(HR.at[g, d - 1], h_sems[(g, d)])
+            h = h + HR[g, d - 1].astype(F32)
+        a, b = act_grad(h, SVP[g, :, pl.ds(0, HQ)], SVP[g, :, pl.ds(HQ, HQ)])
+        G[g, y, 0] = a
+        G[g, y, 1] = b
         for d in (1, -1):
             rs = rsem_new()
-            g_sems[(g, e, d)] = rs
-            send(G.at[g, e, y], G.at[g, e, y], rs, ydev(d))
-
-    def relay(g, e):
+            g_sems[(g, d)] = rs
+            send(G.at[g, y], G.at[g, y], rs, ydev(d))
+
+    def relay(g):
         for k, d in ((0, 1), (1, -1)):
-            piece = G.at[g, e, yof(-d)]
-            recv(piece, g_sems[(g, e, d)])
+            piece = G.at[g, yof(-d)]
+            recv(piece, g_sems[(g, d)])
             rs = rsem_new()
-            g_sems[(g, e, 2, k)] = rs
+            g_sems[(g, 2, k)] = rs
             send(piece.at[k], piece.at[k], rs, ydev(d))
 
     def outward(g):
+        for k in range(2):
+            recv(G.at[g, yof(2), k], g_sems[(g, 2, k)])
+        left = jnp.concatenate([G[g, q, k] for q in range(NY) for k in range(2)], axis=1)
+        parts = []
         for e in range(NE):
-            for k in range(2):
-                recv(G.at[g, e, yof(2), k], g_sems[(g, e, 2, k)])
-            left = jnp.concatenate([G[g, e, q, k] for q in range(NY) for k in range(2)], axis=1)
             right = jnp.concatenate([W2[e, q, k] for q in range(NY) for k in range(2)], axis=1)
-            OB[g, e] = dot_nt(left, right).astype(BF).reshape(PEERS, SROWS, DQ)
+            parts.append(dot_nt(left, right))
+        OB[g] = jnp.where(second(DQ), parts[1], parts[0]).astype(BF).reshape(PEERS, PR, DQ)
         for d in range(1, PEERS):
             rs = rsem_new()
             b_sems[(g, d)] = rs
             peer = peer_of(d)
-            send(OB.at[g, :, peer], BK.at[g, pl.ds(me * NE, NE)], rs, pdev(peer))
-        return local(OB.at[g, :, me], BK.at[g, pl.ds(me * NE, NE)])
+            send(OB.at[g, peer], BK.at[g, me], rs, pdev(peer))
+        keep[g + GROUPS] = local(OB.at[g, me], BK.at[g, me])
 
     def combine(g):
-        keep[g + 2].wait()
+        keep[g + GROUPS].wait()
         for d in range(1, PEERS):
-            recv(BK.at[g, pl.ds(peer_of(-d) * NE, NE)], b_sems[(g, d)])
-        rows = BK[g].reshape(QN * SROWS, DQ)
-        n = 4
-        size = SPAN * TOK // n
-        for i in range(n):
-            at = pl.ds(i * size, size)
-            got = dot_nn(WTH[g, at, :], rows) + dot_nn(WTL[g, at, :], rows)
-            PT[g * SPAN + i * (SPAN // n):g * SPAN + (i + 1) * (SPAN // n)] = got.reshape(SPAN // n, TOK, DQ)
+            recv(BK.at[g, peer_of(-d)], b_sems[(g, d)])
+        rows = BK[g].reshape(ROWS, DQ)
+        got = dot_nn(WTH[g], rows) + dot_nn(WTL[g], rows)
+        PT[g * SPAN:(g + 1) * SPAN] = got.reshape(SPAN, TOK, DQ)
 
     s_sems = {}
 
@@ -360,32 +350,12 @@
             if d == 0:
                 SHO[...] = part
             else:
-                SP[d - 1] = part
+                SP[d - 1] = part.astype(BF)
 
     def shared_sum():
         for d in range(1, NY):
             s_sems[d] = rsem_new()
             send(SP.at[d - 1], SR.at[d - 1], s_sems[d], ydev(d))
-
-    hidden(0)
-    weigh(1)
-    activate(0, 0)
-    hidden(1)
-    spread_shared()
-    activate(1, 0)
-    activate(1, 1)
-    relay(0, 0)
-    activate(0, 1)
-    relay(1, 0)
-    relay(1, 1)
-    cp_w2.wait()
-    for d in range(1, NY):
-        recv(W2.at[:, yof(-d)], w2_sems[d])
-    keep[3] = outward(1)
-    relay(0, 1)
-    shared_products()
-    keep[2] = outward(0)
-    shared_sum()
 
     z_sems = {}
 
@@ -408,17 +378,73 @@
                     zdev(1 if direction == 0 else -1),
                 )
 
+    cp_x.wait()
+    for s in range(1, 9):
+        for i in range(AGC + 2):
+            for direction in range(2):
+                ref = ag_ref(s, direction, i)
+                if ref is None:
+                    continue
+                recv(ref, ag_sems[(s, direction, i)])
+                if s < 8:
+                    ag_send(s + 1, direction, i)
+        if s == 1:
+            permute_saved(0)
+        if s == 2:
+            keep[0] = select(0)
+            send_w2()
+        if s == 3:
+            permute_saved(1)
+        if s == 4:
+            keep[1] = select(1)
+        if s == 5:
+            wait_w1()
+            hidden(0)
+        if s == 6:
+            keep[2] = select(2)
+        if s == 7:
+            hidden(1)
+    keep[3] = select(3)
+    hidden(2)
+    permute_saved(3)
+    weigh(3)
+    hidden(3)
+    spread_shared()
+    permute_saved(2)
+    activate(3)
+    weigh(2)
+    weigh(1)
+    relay(3)
+    activate(2)
+    wait_w2()
+    outward(3)
+    relay(2)
+    activate(1)
+    weigh(0)
+    shared_products()
+    combine(3)
+    rs_step(1)
+    outward(2)
+    relay(1)
+    activate(0)
+    shared_sum()
+    rs_step(2)
+    combine(2)
+    rs_step(3)
+    outward(1)
+    relay(0)
+    rs_step(4)
     combine(1)
-    rs_step(1)
-    rs_step(2)
-    rs_step(3)
+    rs_step(5)
+    outward(0)
+    rs_step(6)
     combine(0)
-    for s in range(4, 9):
-        rs_step(s)
+    rs_step(7)
+    rs_step(8)
     total = PT[HOME] + SHO[...]
     for d in range(1, NY):
         recv(SR.at[d - 1], s_sems[d])
-        total = total + SR[d - 1]
+        total = total + SR[d - 1].astype(F32)
     PT[HOME] = total
     for i in range(RSC):
         rows = pl.ds(i * RSR, RSR)
@@ -442,31 +468,31 @@
         pltpu.VMEM((NZ, TOK, DQ), BF),
         pltpu.VMEM((NZ, 24, TOK), F32),
         pltpu.VMEM((3, NX, NZ, NC, 16, HQ), BF),
-        pltpu.VMEM((QN * SROWS, SPAN * TOK), BF),
-        pltpu.VMEM((GROUPS, SPAN * TOK, QN * SROWS), BF),
-        pltpu.VMEM((GROUPS, SPAN * TOK, QN * SROWS), BF),
-        pltpu.VMEM((GROUPS, QN, SROWS, DQ), BF),
-        pltpu.VMEM((GROUPS, NE, PEERS, SROWS, DQ), BF),
+        pltpu.VMEM((ROWS, SPAN * TOK), BF),
+        pltpu.VMEM((GROUPS, SPAN * TOK, ROWS), BF),
+        pltpu.VMEM((GROUPS, SPAN * TOK, ROWS), BF),
+        pltpu.VMEM((GROUPS, PEERS, PR, DQ), BF),
+        pltpu.VMEM((GROUPS, PEERS, PR, DQ), BF),
         pltpu.VMEM((NE, NY * HQ, DQ), BF),
         pltpu.VMEM((NE, NY, 2, DQ, HQ), BF),
         pltpu.VMEM((slots, 2 * NE * HQ), BF),
-        pltpu.VMEM((GROUPS, ROWS, 2 * NE * HQ), BF),
-        pltpu.VMEM((GROUPS, NE, ROWS, HQ), F32),
-        pltpu.VMEM((GROUPS, NE, NY - 1, ROWS, HQ), BF),
-        pltpu.VMEM((GROUPS, NE, NY - 1, ROWS, HQ), BF),
-        pltpu.VMEM((GROUPS, NE, NY, 2, ROWS, HQ), BF),
-        pltpu.VMEM((GROUPS, NE, PEERS, SROWS, DQ), BF),
-        pltpu.VMEM((GROUPS, QN, SROWS, DQ), BF),
+        pltpu.VMEM((GROUPS, ROWS, 2 * HQ), BF),
+        pltpu.VMEM((GROUPS, ROWS, HQ), F32),
+        pltpu.VMEM((GROUPS, NY - 1, ROWS, HQ), BF),
+        pltpu.VMEM((GROUPS, NY - 1, ROWS, HQ), BF),
+        pltpu.VMEM((GROUPS, NY, 2, ROWS, HQ), BF),
+        pltpu.VMEM((GROUPS, PEERS, PR, DQ), BF),
+        pltpu.VMEM((GROUPS, PEERS, PR, DQ), BF),
         pltpu.VMEM((NZ, TOK, DQ), F32),
         pltpu.VMEM((2, 8, TOK, DQ), BF),
         pltpu.VMEM((2, 8, TOK, DQ), BF),
         pltpu.VMEM((TOK, NX * DQ), BF),
         pltpu.VMEM((TOK, DQ), F32),
-        pltpu.VMEM((NY - 1, TOK, DQ), F32),
-        pltpu.VMEM((NY - 1, TOK, DQ), F32),
-        pltpu.SemaphoreType.DMA((228,)),
-        pltpu.SemaphoreType.DMA((228,)),
-        pltpu.SemaphoreType.DMA((16,)),
+        pltpu.VMEM((NY - 1, TOK, DQ), BF),
+        pltpu.VMEM((NY - 1, TOK, DQ), BF),
+        pltpu.SemaphoreType.DMA((252,)),
+        pltpu.SemaphoreType.DMA((252,)),
+        pltpu.SemaphoreType.DMA((20,)),
     ]
     return pl.pallas_call(
         kernel,

time: 138 us -> 127 us (0.920); the launches traced: 137 us -> 127 us
  Pallas kernels: 135 us -> 126 us
    pallas_call x1, Pallas kernels: 135 us -> 126 us  [shards(): pl.pallas_call(kernel, out_shape=jax.ShapeDtypeStruct((TOK, DQ), BF), in_...]
where the time goes in v3:
time: 127 us
  Pallas kernels  126 us (99%)
  local copies, waits for them, and re-layouts  1.57 us (1%)
    pallas_call x1, Pallas kernels, shards(): pl.pallas_call(kernel, out_shape=jax.ShapeDtypeStruct((TOK, DQ), BF), in_...  126 us

profile of v3, /device:TPU:1, one launch (start us, length us, event | category | flops | bytes accessed | tf_op | source)
XLA Modules:
  0.0 127.3 jit_solution(14825109439058328118)
XLA Ops:
  0.0 125.7 %shard_map.91 = bf16[128,512]{1,0:T(8,128)(2,1)} custom-call(bf16[128,2048]{1,0:T(8,128)(2,1)} %x_in.1, s32[10,128]{1,0:T(8,128)} %bitcast.3, f32[10,128]{1,0:T(8,128)} %bitcast.4, bf16[16,128]{1,0:T(8,128)(2,1)} %bitcast.5, bf16[2,16,128]{2,1,0:T(8,128)(2,1)} %sgu.1, bf16[2,2,768,128]{3,2,1,0:T(8,128)(2,1)} %saved.1, bf16[2,2,2048,128]{3,2,1,0:T(8,128)(2,1)} %gu.1, ...), custom_call_target="tpu_custom_call" | custom-call | flops 8000000000 | bytes 8000000 | tf_op jit(solution)/shard_map/pallas_call | solution.py:497
  125.7 1.6 %copy.11 = bf16[128,512]{1,0:T(8,128)(2,1)} copy(bf16[128,512]{1,0:T(8,128)(2,1)} %shard_map.91) | data formatting | bytes 262144

commit v4 on v3

--- a/solution.py
+++ b/solution.py
@@ -26,7 +26,7 @@
 HOME = 0
 AGC = 4
 AGR = TOK // AGC
-RSC = 4
+RSC = 2
 RSR = TOK // RSC
 OFFS = (0, 1, -1, 2, -2, 3, -3, 4, -4, 5, -5, 6, -6, 7, -7, 8)
 
@@ -421,13 +421,11 @@
     relay(2)
     activate(1)
     weigh(0)
-    shared_products()
     combine(3)
     rs_step(1)
     outward(2)
     relay(1)
     activate(0)
-    shared_sum()
     rs_step(2)
     combine(2)
     rs_step(3)
@@ -437,6 +435,8 @@
     combine(1)
     rs_step(5)
     outward(0)
+    shared_products()
+    shared_sum()
     rs_step(6)
     combine(0)
     rs_step(7)

time: 127 us -> 127 us (level)
  no operation moved by 1% of the time
where the time goes in v4:
time: 127 us
  Pallas kernels  126 us (99%)
  local copies, waits for them, and re-layouts  1.57 us (1%)
    pallas_call x1, Pallas kernels, shards(): pl.pallas_call(kernel, out_shape=jax.ShapeDtypeStruct((TOK, DQ), BF), in_...  126 us

profile of v4, /device:TPU:1, one launch (start us, length us, event | category | flops | bytes accessed | tf_op | source)
XLA Modules:
  0.0 127.3 jit_solution(15973831558159643359)
XLA Ops:
  0.0 125.7 %shard_map.91 = bf16[128,512]{1,0:T(8,128)(2,1)} custom-call(bf16[128,2048]{1,0:T(8,128)(2,1)} %x_in.1, s32[10,128]{1,0:T(8,128)} %bitcast.3, f32[10,128]{1,0:T(8,128)} %bitcast.4, bf16[16,128]{1,0:T(8,128)(2,1)} %bitcast.5, bf16[2,16,128]{2,1,0:T(8,128)(2,1)} %sgu.1, bf16[2,2,768,128]{3,2,1,0:T(8,128)(2,1)} %saved.1, bf16[2,2,2048,128]{3,2,1,0:T(8,128)(2,1)} %gu.1, ...), custom_call_target="tpu_custom_call" | custom-call | flops 8000000000 | bytes 8000000 | tf_op jit(solution)/shard_map/pallas_call | solution.py:497
  125.7 1.6 %copy.11 = bf16[128,512]{1,0:T(8,128)(2,1)} copy(bf16[128,512]{1,0:T(8,128)(2,1)} %shard_map.91) | data formatting | bytes 262144
